TPU v7x, 32 devices: a whole 2x2x4 slice. The times are simulated.
32 devices in a mesh: groups: 2 (over x), col: 16 (over z, y, core).
Axes of the slice: x: 2, y: 2, z: 4, core: 2. Of those that a mesh axis runs over, the one named last changes fastest.
Arguments:
- query_grad: bfloat16 [16384, 14336], P('groups', 'col'), parts along dimension 0, may hold values from -6 to 6
- out_basis: bfloat16 [16384, 2048], P(('groups', 'col')), parts along dimension 0, may hold values from -0.09375 to 0.09375
- in_basis: bfloat16 [28672, 384], P(('groups', 'col')), parts along dimension 0, may hold values from -0.0625 to 0.0625
- eigenvalues: float32 [4096, 384], P(('groups', 'col')), parts along dimension 0, may hold values from 0.05 to 20
- damping: float32 [2], P('groups'), parts along dimension 0, may hold values from 0.5 to 2
Outputs:
- ihvp: bfloat16 [16384, 14336], P('groups', 'col'), parts along dimension 0
There are 2 independent parts, one for each index of `groups`. A program takes and returns all parts, laid end to end along the dimension named above; each array names one. Nothing has to cross between parts.
All inputs are finite; a program needn't handle non-finite values.
Results may differ from a plain program's by a relative error of at most 0.004.
Values may be sent and summed in bfloat16 or wider, within the bound.
A program may use at most 128 MiB of HBM per device.

v0:
```python
import jax
import jax.numpy as jnp
from jax import lax
from jax.sharding import PartitionSpec as P


def on_device(query_grad, out_basis, in_basis, eigenvalues, damping):
    damp_value = damping[0]
    projected = lax.psum_scatter(
        jnp.dot(query_grad, in_basis, preferred_element_type=jnp.float32),
        "col",
        scatter_dimension=0,
        tiled=True,
    ).astype(jnp.bfloat16)
    partial_coords = lax.dot_general(
        out_basis, projected, (((0,), (0,)), ((), ())), preferred_element_type=jnp.float32
    )
    coord_share = lax.psum_scatter(partial_coords, "col", scatter_dimension=0, tiled=True)
    factor = 1.0 / (eigenvalues + damp_value) - 1.0 / damp_value
    scaled_share = (coord_share * factor).astype(jnp.bfloat16)
    scaled = lax.all_gather(scaled_share, "col", axis=0, tiled=True)
    lifted = jnp.dot(out_basis, scaled, preferred_element_type=jnp.float32).astype(jnp.bfloat16)
    restored = lax.dot_general(
        lax.all_gather(lifted, "col", axis=0, tiled=True),
        in_basis,
        (((1,), (1,)), ((), ())),
        preferred_element_type=jnp.float32,
    )
    return (query_grad.astype(jnp.float32) / damp_value + restored).astype(jnp.bfloat16)


def solution(mesh):
    in_specs = (
        P("groups", "col"),
        P(("groups", "col"), None),
        P(("groups", "col"), None),
        P(("groups", "col"), None),
        P("groups"),
    )
    out_specs = P("groups", "col")
    return jax.shard_map(
        on_device, mesh=mesh, in_specs=in_specs, out_specs=out_specs, check_vma=False
    )
```

profile of v0, /device:TPU:0, one launch (start us, length us, event | category | flops | bytes accessed | tf_op | source)
XLA Modules:
  0.0 359.7 jit_solution(16717528067151458415)
XLA Ops:
  6.5 0.0 copy-start
  6.5 0.0 reduce-scatter.3.cloned.1.call-start
  6.5 14.6 %fusion.2 = f32[8192,384]{1,0:T(8,128)} fusion(bf16[8192,896]{1,0:T(8,128)(2,1)} %param.5, bf16[896,384]{1,0:T(8,128)(2,1)} %param.7), kind=kOutput, calls=%fused_computation.6 | convolution fusion | flops 5637144576 | bytes 27951104 | tf_op jit(solution)/shard_map/dot_general | solution.py:10
  21.1 0.0 reduce-scatter.3.cloned.1.call-update
  21.1 0.0 copy-start.1
  21.1 0.0 reduce-scatter.5.cloned.1.call-start
  21.2 137.5 %reduce-scatter.3.cloned.1.call-done = f32[512,384]{1,0:T(8,128)} async-done(((f32[8192,384]{1,0:T(8,128)}), f32[512,384]{1,0:T(8,128)}) %reduce-scatter.3.cloned.1.call-update) | async-done | bytes 786448 | tf_op jit(solution)/shard_map/reduce_scatter | solution.py:9
  158.7 0.0 copy-done
  158.7 4.1 %convolution_bitcast_fusion = f32[2048,384]{1,0:T(8,128)} fusion(bf16[512,2048]{1,0:T(8,128)(2,1)S(1)} %copy-done, f32[512,384]{1,0:T(8,128)} %reduce-scatter.3.cloned.1.call-done), kind=kOutput, calls=%fused_computation.1 | convolution fusion | flops 805502976 | bytes 6029312 | tf_op jit(solution)/shard_map/dot_general | solution.py:15
  162.8 0.0 copy-start.2
  162.8 0.0 reduce-scatter.5.cloned.1.call-update
  162.8 0.0 all-gather.3.cloned.1.call-start
  163.6 64.7 %reduce-scatter.5.cloned.1.call-done = f32[128,384]{1,0:T(8,128)} async-done(((f32[2048,384]{1,0:T(8,128)}), f32[128,384]{1,0:T(8,128)}) %reduce-scatter.5.cloned.1.call-update) | async-done | bytes 196624 | tf_op jit(solution)/shard_map/reduce_scatter | solution.py:18
  228.3 0.0 copy-done.1
  228.3 1.6 multiply_convert_fusion
  229.9 0.0 all-gather.3.cloned.1.call-update
  229.9 0.0 all-gather.5.cloned.1.call-start
  230.0 39.3 %all-gather.3.cloned.1.call-done = bf16[2048,384]{1,0:T(8,128)(2,1)} async-done(((bf16[128,384]{1,0:T(8,128)(2,1)}), bf16[2048,384]{1,0:T(8,128)(2,1)}) %all-gather.3.cloned.1.call-update) | async-done | bytes 1572880 | tf_op jit(solution)/shard_map/all_gather | solution.py:21
  269.3 3.2 fusion
  272.5 0.0 all-gather.5.cloned.1.call-update
  272.5 64.7 %all-gather.5.cloned.1.call-done = bf16[8192,384]{0,1:T(8,128)(2,1)} async-done(((bf16[512,384]{0,1:T(8,128)(2,1)}), bf16[8192,384]{0,1:T(8,128)(2,1)}) %all-gather.5.cloned.1.call-update) | async-done | bytes 6291472 | tf_op jit(solution)/shard_map/all_gather | solution.py:24
  337.2 0.0 copy-done.2
  337.2 15.9 %add_convert_fusion = bf16[8192,896]{1,0:T(8,128)(2,1)} fusion(bf16[8192,896]{1,0:T(8,128)(2,1)} %param.5, bf16[8192,384]{0,1:T(8,128)(2,1)} %all-gather.5.cloned.1.call-done, bf16[896,384]{1,0:T(8,128)(2,1)S(1)} %copy-done.2, f32[]{:T(128)} %bitcast.12), kind=kOutput, calls=%fused_computation | convolution fusion | flops 5666504704 | bytes 36339716 | tf_op jit(solution)/shard_map/dot_general | solution.py:23
Async XLA Ops:
  6.5 152.2 %copy-start = (bf16[512,2048]{1,0:T(8,128)(2,1)S(1)}, bf16[512,2048]{1,0:T(8,128)(2,1)}, u32[]{:S(2)}) copy-start(bf16[512,2048]{1,0:T(8,128)(2,1)} %param.6) | copy-start | bytes 6291460
  6.5 152.2 %reduce-scatter.3.cloned.1.call-start = ((), (), s32[]{:S(2)}) async-start(), calls=%async_computation.2 | async-start | bytes 13369344 | tf_op jit(solution)/shard_map/reduce_scatter | solution.py:9
  21.1 207.2 %copy-start.1 = (f32[128,384]{1,0:T(8,128)S(1)}, f32[128,384]{1,0:T(8,128)}, u32[]{:S(2)}) copy-start(f32[128,384]{1,0:T(8,128)} %param.8) | copy-start | bytes 589828
  21.1 207.2 %reduce-scatter.5.cloned.1.call-start = ((), (), s32[]{:S(2)}) async-start(), calls=%async_computation.3 | async-start | bytes 3342336 | tf_op jit(solution)/shard_map/reduce_scatter | solution.py:18
  162.8 174.4 %copy-start.2 = (bf16[896,384]{1,0:T(8,128)(2,1)S(1)}, bf16[896,384]{1,0:T(8,128)(2,1)}, u32[]{:S(2)}) copy-start(bf16[896,384]{1,0:T(8,128)(2,1)} %param.7) | copy-start | bytes 2064388
  162.8 106.5 %all-gather.3.cloned.1.call-start = ((), (), s32[]{:S(2)}) async-start(), calls=%async_computation.4 | async-start | bytes 1671168 | tf_op jit(solution)/shard_map/all_gather | solution.py:21
  229.9 107.3 %all-gather.5.cloned.1.call-start = ((), (), s32[]{:S(2)}) async-start(), calls=%async_computation.5 | async-start | bytes 6684672 | tf_op jit(solution)/shard_map/all_gather | solution.py:24
Sparse Core Ops, SparseCore 0:
  21.2 137.4 reduce-scatter.2
  162.9 65.3 reduce-scatter.4
  230.6 38.6 all-gather.2
  272.6 64.5 all-gather.4
where the time goes:
time: 360 us
  waiting for transfers between devices  306 us (85%)
  matrix products  37.8 us (10%)
  between operations  13.9 us (4%)
    reduce_scatter x1, waiting for transfers between devices, on_device(): lax.psum_scatter(jnp.dot(query_grad, in_basis, preferred_element_type=jnp...  138 us
    all_gather x1, waiting for transfers between devices, on_device(): lax.all_gather(lifted, 'col', axis=0, tiled=True)  64.7 us
    reduce_scatter x1, waiting for transfers between devices, on_device(): lax.psum_scatter(partial_coords, 'col', scatter_dimension=0, tiled=True)  64.7 us
    all_gather x1, waiting for transfers between devices, on_device(): scaled = lax.all_gather(scaled_share, 'col', axis=0, tiled=True)  39.3 us
    dot_general x1, matrix products, on_device(): lax.dot_general(lax.all_gather(lifted, 'col', axis=0, tiled=True), in_bas...  15.9 us
    dot_general x1, matrix products, on_device(): jnp.dot(query_grad, in_basis, preferred_element_type=jnp.float32)  14.6 us
  transfers between devices with their start and end apart: 4, of which 4 were waited for; matrix products, arithmetic and copies ran while one was open for 0% of the time, Pallas kernels for 0%

commit v1 on v0

v1 whole, which is shorter than its diff:
```python
import functools

import jax
import jax.numpy as jnp
from jax import lax
from jax.experimental import pallas as pl
from jax.experimental.pallas import tpu as pltpu
from jax.sharding import PartitionSpec as P

MESH = pl.DeviceIdType.MESH
SLOTS = 4


def rows_of(block, rows):
    return pl.ds(pl.multiple_of(block * rows, rows), rows)


def tile_of(rows):
    return 256 if rows % 256 == 0 else rows


class Place:
    def __init__(self, n):
        self.n = n
        self.depths = n // 4
        me = lax.axis_index("col")
        self.me = me
        self.z = me // 4
        self.y = (me // 2) % 2
        self.c = me % 2

    def index(self, z, y, c):
        return z * 4 + y * 2 + c

    def core_peer(self):
        return self.index(self.z, self.y, 1 - self.c)

    def side_peer(self):
        return self.index(self.z, 1 - self.y, self.c)

    def depth_peer(self, step):
        return self.index((self.z + step) % self.depths, self.y, self.c)


def remote(src, dst, send_sem, recv_sem, target):
    return pltpu.make_async_remote_copy(
        src_ref=src,
        dst_ref=dst,
        send_sem=send_sem,
        recv_sem=recv_sem,
        device_id={"col": target},
        device_id_type=MESH,
    )


def reduce_scatter(place, rows, produce, interlude, bufs):
    own, kept, csend, crecv, ysend, yrecv, zsend, zrecv, cs, cr, ys, yr, zs, zr = bufs
    nz = place.depths
    tile = tile_of(rows)

    def core_copy(i):
        return remote(csend.at[i], crecv.at[i], cs.at[i], cr.at[i], place.core_peer())

    def side_copy(k):
        return remote(ysend.at[k], yrecv.at[k], ys.at[k], yr.at[k], place.side_peer())

    def depth_copy(k):
        return remote(zsend.at[k], zrecv.at[k], zs.at[k], zr.at[k], place.depth_peer(k + 1))

    def tiles(body):
        @pl.loop(0, rows // tile)
        def _(t):
            body(pl.ds(pl.multiple_of(t * tile, tile), tile))

    produce(0, csend.at[0])
    core_copy(0).start()

    @pl.loop(0, nz)
    def _(k):
        produce(2 * k + 1, own)

        @pl.when(k + 1 < nz)
        def _():
            produce(2 * k + 2, csend.at[k + 1])
            core_copy(k + 1).start()

        core_copy(k).wait_recv()

        def add(r):
            ysend[k, r, :] = (own[r, :] + crecv[k, r, :].astype(jnp.float32)).astype(jnp.bfloat16)

        tiles(add)
        side_copy(k).start()

    @pl.loop(0, nz)
    def _(k):
        produce(2 * nz + 2 * k, csend.at[nz + k])
        core_copy(nz + k).start()
        produce(2 * nz + 2 * k + 1, kept.at[k])

    interlude()

    def total(k, r):
        return (
            kept[k, r, :]
            + crecv[nz + k, r, :].astype(jnp.float32)
            + yrecv[k, r, :].astype(jnp.float32)
        )

    @pl.loop(0, nz - 1)
    def _(k):
        core_copy(nz + k).wait_recv()
        side_copy(k).wait_recv()

        def add(r):
            zsend[k, r, :] = total(k, r).astype(jnp.bfloat16)

        tiles(add)
        depth_copy(k).start()

    core_copy(2 * nz - 1).wait_recv()
    side_copy(nz - 1).wait_recv()

    def last(r):
        own[r, :] = total(nz - 1, r)

    tiles(last)

    @pl.loop(0, nz - 1)
    def _(k):
        depth_copy(k).wait_recv()

        def add(r):
            own[r, :] += zrecv[k, r, :].astype(jnp.float32)

        tiles(add)

    @pl.loop(0, 2 * nz)
    def _(i):
        core_copy(i).wait_send()

    @pl.loop(0, nz)
    def _(k):
        side_copy(k).wait_send()

    @pl.loop(0, nz - 1)
    def _(k):
        depth_copy(k).wait_send()


def all_gather(place, rows, full, bufs):
    cs, cr, ys, yr, zs, zr = bufs
    nz = place.depths

    def at(block):
        return full.at[rows_of(block, rows)]

    def depth_copy(k, source_z):
        block = at(place.index(source_z, place.y, place.c))
        return remote(block, block, zs.at[k], zr.at[k], place.depth_peer(k))

    def side_copy(k, side):
        block = at(place.index((place.z - k + nz) % nz, side, place.c))
        return remote(block, block, ys.at[k], yr.at[k], place.side_peer())

    def core_copy(i, k, side, core):
        block = at(place.index((place.z - k + nz) % nz, side, core))
        return remote(block, block, cs.at[i], cr.at[i], place.core_peer())

    @pl.loop(1, nz)
    def _(k):
        depth_copy(k, place.z).start()

    @pl.loop(0, nz)
    def _(k):
        @pl.when(k > 0)
        def _():
            depth_copy(k, (place.z - k + nz) % nz).wait_recv()

        side_copy(k, place.y).start()
        core_copy(k, k, place.y, place.c).start()

    @pl.loop(0, nz)
    def _(k):
        side_copy(k, 1 - place.y).wait_recv()
        core_copy(nz + k, k, 1 - place.y, place.c).start()

    @pl.loop(0, nz)
    def _(k):
        core_copy(k, k, place.y, 1 - place.c).wait_recv()
        core_copy(nz + k, k, 1 - place.y, 1 - place.c).wait_recv()

    @pl.loop(1, nz)
    def _(k):
        depth_copy(k, place.z).wait_send()

    @pl.loop(0, nz)
    def _(k):
        side_copy(k, place.y).wait_send()
        core_copy(k, k, place.y, place.c).wait_send()
        core_copy(nz + k, k, 1 - place.y, place.c).wait_send()


def lift_kernel(
    n, query, out_basis, in_basis, eigenvalues, damping, lifted,
    slots, basis, turned, projected, scaled, slot_sems, basis_sem, *rest
):
    place = Place(n)
    nz = place.depths
    first, second, gather_scaled, gather_lifted = rest[:14], rest[14:28], rest[28:34], rest[34:40]
    rows = projected.shape[0]
    share = eigenvalues.shape[0]
    steps = 4 * nz

    def block_at(s):
        half = s // (2 * nz)
        k = (s % (2 * nz)) // 2
        side = (place.y + 1 + half) % 2
        core = (place.c + 1 + s) % 2
        return place.index((place.z + k + 1) % nz, side, core)

    def query_copy(s):
        return pltpu.make_async_copy(
            query.at[rows_of(block_at(s), rows)], slots.at[s % SLOTS], slot_sems.at[s % SLOTS]
        )

    basis_copy = pltpu.make_async_copy(out_basis, basis, basis_sem)

    @pl.loop(0, SLOTS - 1)
    def _(s):
        query_copy(s).start()

    barrier = pltpu.get_barrier_semaphore()
    for peer in (place.core_peer(), place.side_peer()):
        pl.semaphore_signal(barrier, inc=1, device_id={"col": peer}, device_id_type=MESH)

    @pl.loop(1, nz)
    def _(k):
        pl.semaphore_signal(
            barrier, inc=1, device_id={"col": place.depth_peer(k)}, device_id_type=MESH
        )

    pl.semaphore_wait(barrier, nz + 1)

    tile = tile_of(rows)

    def project(s, out):
        query_copy(s).wait()

        @pl.when(s + SLOTS - 1 < steps)
        def _():
            query_copy(s + SLOTS - 1).start()

        @pl.loop(0, rows // tile)
        def _(t):
            r = pl.ds(pl.multiple_of(t * tile, tile), tile)
            out[r, :] = jnp.dot(
                slots[s % SLOTS, r, :], in_basis[...], preferred_element_type=jnp.float32
            ).astype(out.dtype)

    basis_copy.start()

    def turn():
        basis_copy.wait()
        width = 256
        for j in range(basis.shape[1] // width):
            turned[j * width : (j + 1) * width, :] = basis[:, j * width : (j + 1) * width].T

    reduce_scatter(place, rows, project, turn, first)
    projected[...] = first[0][...].astype(jnp.bfloat16)

    def rotate(s, out):
        out[...] = jnp.dot(
            turned[rows_of(block_at(s), share), :],
            projected[...],
            preferred_element_type=jnp.float32,
        ).astype(out.dtype)

    reduce_scatter(place, share, rotate, lambda: None, second)
    damp_value = damping[...]
    factor = 1.0 / (eigenvalues[...] + damp_value) - 1.0 / damp_value
    scaled[rows_of(place.me, share), :] = (second[0][...] * factor).astype(jnp.bfloat16)
    all_gather(place, share, scaled, gather_scaled)

    @pl.loop(0, rows // tile)
    def _(t):
        r = pl.ds(pl.multiple_of(t * tile, tile), tile)
        o = pl.ds(pl.multiple_of(place.me * rows + t * tile, tile), tile)
        lifted[o, :] = jnp.dot(
            basis[r, :], scaled[...], preferred_element_type=jnp.float32
        ).astype(jnp.bfloat16)

    all_gather(place, rows, lifted, gather_lifted)


def scatter_scratch(nz, rows, width):
    block = (rows, width)
    dma = pltpu.SemaphoreType.DMA
    return [
        pltpu.VMEM(block, jnp.float32),
        pltpu.VMEM((nz, *block), jnp.float32),
        pltpu.VMEM((2 * nz, *block), jnp.bfloat16),
        pltpu.VMEM((2 * nz, *block), jnp.bfloat16),
        pltpu.VMEM((nz, *block), jnp.bfloat16),
        pltpu.VMEM((nz, *block), jnp.bfloat16),
        pltpu.VMEM((nz - 1, *block), jnp.bfloat16),
        pltpu.VMEM((nz - 1, *block), jnp.bfloat16),
        dma((2 * nz,)),
        dma((2 * nz,)),
        dma((nz,)),
        dma((nz,)),
        dma((nz - 1,)),
        dma((nz - 1,)),
    ]


def gather_scratch(nz):
    dma = pltpu.SemaphoreType.DMA
    return [dma((2 * nz,)), dma((2 * nz,)), dma((nz,)), dma((nz,)), dma((nz,)), dma((nz,))]


def lift(n, query_grad, out_basis, in_basis, eigenvalues, damping):
    nz = n // 4
    height, inner = query_grad.shape
    rows, kept = out_basis.shape
    width = in_basis.shape[1]
    share = eigenvalues.shape[0]
    vmem = pl.BlockSpec(memory_space=pltpu.VMEM)
    hbm = pl.BlockSpec(memory_space=pl.ANY)
    flops = 2 * height * inner * width + 4 * rows * kept * width
    return pl.pallas_call(
        functools.partial(lift_kernel, n),
        out_shape=jax.ShapeDtypeStruct((height, width), jnp.bfloat16),
        in_specs=[hbm, hbm, vmem, vmem, vmem],
        out_specs=vmem,
        scratch_shapes=[
            pltpu.VMEM((SLOTS, rows, inner), jnp.bfloat16),
            pltpu.VMEM((rows, kept), jnp.bfloat16),
            pltpu.VMEM((kept, rows), jnp.bfloat16),
            pltpu.VMEM((rows, width), jnp.bfloat16),
            pltpu.VMEM((kept, width), jnp.bfloat16),
            pltpu.SemaphoreType.DMA((SLOTS,)),
            pltpu.SemaphoreType.DMA,
            *scatter_scratch(nz, rows, width),
            *scatter_scratch(nz, share, width),
            *gather_scratch(nz),
            *gather_scratch(nz),
        ],
        compiler_params=pltpu.CompilerParams(
            collective_id=0, has_side_effects=True, vmem_limit_bytes=52 * 2**20
        ),
        cost_estimate=pl.CostEstimate(
            flops=flops, bytes_accessed=2 * height * inner, transcendentals=0
        ),
    )(query_grad, out_basis, in_basis, eigenvalues, damping.reshape(1, 1))


def on_device(n, query_grad, out_basis, in_basis, eigenvalues, damping):
    damp_value = damping[0]
    lifted = lift(n, query_grad, out_basis, in_basis, eigenvalues, damping)
    restored = lax.dot_general(
        lifted, in_basis, (((1,), (1,)), ((), ())), preferred_element_type=jnp.float32
    )
    return (query_grad.astype(jnp.float32) / damp_value + restored).astype(jnp.bfloat16)


def solution(mesh):
    in_specs = (
        P("groups", "col"),
        P(("groups", "col"), None),
        P(("groups", "col"), None),
        P(("groups", "col"), None),
        P("groups"),
    )
    out_specs = P("groups", "col")
    return jax.shard_map(
        functools.partial(on_device, mesh.shape["col"]),
        mesh=mesh,
        in_specs=in_specs,
        out_specs=out_specs,
        check_vma=False,
    )
```

time: 360 us -> 164 us (0.46)
  waiting for transfers between devices: 306 us -> 0 us
  Pallas kernels: 0 us -> 143 us
  matrix products: 37.8 us -> 15.8 us
  between operations: 13.9 us -> 0.68 us
    reduce_scatter x2 -> x0, waiting for transfers between devices: 202 us -> none  [the longest x1 138 us: on_device(): lax.psum_scatter(jnp.dot(query_grad, in_basis, preferred_element_type=jnp...]
    pallas_call x0 -> x1, Pallas kernels: none -> 143 us  [lift(): pl.pallas_call(functools.partial(lift_kernel, n), out_shape=jax.ShapeDtyp...]
    all_gather x2 -> x0, waiting for transfers between devices: 104 us -> none  [the longest x1 64.7 us: on_device(): lax.all_gather(lifted, 'col', axis=0, tiled=True)]
    dot_general x4 -> x1, matrix products: 37.8 us -> 15.8 us  [on_device(): lax.dot_general(lifted, in_basis, (((1,), (1,)), ((), ())), preferred_ele...]
  transfers between devices with their start and end apart: 4 -> 0, of which waited for: 4 -> 0; matrix products, arithmetic and copies ran while one was open for 0% -> 0% of each run, Pallas kernels for 0% -> 0%
where the time goes in v1:
time: 164 us; the launch traced here: 161 us
  Pallas kernels  143 us (87%)
  matrix products  15.8 us (10%)
  local copies, waits for them, and re-layouts  2.02 us (1%)
    pallas_call x1, Pallas kernels, lift(): pl.pallas_call(functools.partial(lift_kernel, n), out_shape=jax.ShapeDtyp...  143 us
    dot_general x1, matrix products, on_device(): lax.dot_general(lifted, in_basis, (((1,), (1,)), ((), ())), preferred_ele...  15.8 us

profile of v1, /device:TPU:0, one launch (start us, length us, event | category | flops | bytes accessed | tf_op | source)
XLA Modules:
  0.0 161.3 jit_solution(12017314334902987290)
XLA Ops:
  0.7 0.0 copy-start
  0.7 1.1 copy-done
  1.8 0.0 copy-start.2
  1.8 0.9 copy-done.2
  2.7 0.0 copy-start.1
  2.7 142.8 %shard_map.55 = bf16[8192,384]{1,0:T(8,128)(2,1)} custom-call(bf16[8192,896]{1,0:T(8,128)(2,1)} %query.1, bf16[512,2048]{1,0:T(8,128)(2,1)} %out_basis.1, bf16[896,384]{1,0:T(8,128)(2,1)S(1)} %copy-done, f32[128,384]{1,0:T(8,128)S(1)} %copy-done.2, f32[1,1]{1,0:T(1,128)} %bitcast.5.damping), custom_call_target="tpu_custom_call" | custom-call | flops 7247757312 | bytes 14680064 | tf_op jit(solution)/shard_map/pallas_call | solution.py:331
  145.5 0.0 copy-done.1
  145.5 15.8 %add_convert_fusion = bf16[8192,896]{1,0:T(8,128)(2,1)} fusion(bf16[8192,896]{1,0:T(8,128)(2,1)} %query.1, bf16[8192,384]{1,0:T(8,128)(2,1)} %shard_map.55, bf16[896,384]{1,0:T(8,128)(2,1)S(1)} %copy-done.1, f32[]{:T(128)} %bitcast.4), kind=kOutput, calls=%fused_computation | convolution fusion | flops 5666504704 | bytes 36339716 | tf_op jit(solution)/shard_map/dot_general | solution.py:361
Async XLA Ops:
  0.7 1.1 copy-start
  1.8 0.9 copy-start.2
  2.7 142.8 %copy-start.1 = (bf16[896,384]{1,0:T(8,128)(2,1)S(1)}, bf16[896,384]{1,0:T(8,128)(2,1)}, u32[]{:S(2)}) copy-start(bf16[896,384]{1,0:T(8,128)(2,1)} %in_basis.1) | copy-start | bytes 2064388

commit v2 on v1

--- a/solution.py
+++ b/solution.py
@@ -39,7 +39,13 @@
         return self.index(self.z, 1 - self.y, self.c)
 
     def depth_peer(self, step):
-        return self.index((self.z + step) % self.depths, self.y, self.c)
+        return self.index((self.z + step + self.depths) % self.depths, self.y, self.c)
+
+    def depth_at(self, k):
+        z, last = self.z, self.depths - 1
+        low = jnp.where(k < last - z, last - k, k - (last - z))
+        high = jnp.where(k < z, k, last - (k - z))
+        return jnp.where(k == last, z, jnp.where(2 * z < self.depths, low, high))
 
 
 def remote(src, dst, send_sem, recv_sem, target):
@@ -64,8 +70,11 @@
     def side_copy(k):
         return remote(ysend.at[k], yrecv.at[k], ys.at[k], yr.at[k], place.side_peer())
 
-    def depth_copy(k):
-        return remote(zsend.at[k], zrecv.at[k], zs.at[k], zr.at[k], place.depth_peer(k + 1))
+    def depth_copy(k, slot, step):
+        return remote(zsend.at[k], zrecv.at[slot], zs.at[k], zr.at[slot], place.depth_peer(step))
+
+    def arrived(slot):
+        depth_copy(0, slot, 1).wait_recv()
 
     def tiles(body):
         @pl.loop(0, rows // tile)
@@ -112,11 +121,30 @@
         core_copy(nz + k).wait_recv()
         side_copy(k).wait_recv()
 
+        depth = place.depth_at(k)
+        up = depth > place.z
+
+        @pl.when(jnp.where(up, place.z > 0, place.z < nz - 1))
+        def _():
+            arrived(depth)
+
+            def join(r):
+                kept[k, r, :] += zrecv[depth, r, :].astype(jnp.float32)
+
+            tiles(join)
+
         def add(r):
             zsend[k, r, :] = total(k, r).astype(jnp.bfloat16)
 
         tiles(add)
-        depth_copy(k).start()
+
+        @pl.when(up)
+        def _():
+            depth_copy(k, depth, 1).start()
+
+        @pl.when(depth < place.z)
+        def _():
+            depth_copy(k, jnp.where(depth == place.z - 1, nz, depth), -1).start()
 
     core_copy(2 * nz - 1).wait_recv()
     side_copy(nz - 1).wait_recv()
@@ -126,14 +154,21 @@
 
     tiles(last)
 
-    @pl.loop(0, nz - 1)
-    def _(k):
-        depth_copy(k).wait_recv()
+    def finish(slot):
+        arrived(slot)
 
         def add(r):
-            own[r, :] += zrecv[k, r, :].astype(jnp.float32)
+            own[r, :] += zrecv[slot, r, :].astype(jnp.float32)
 
         tiles(add)
+
+    @pl.when(place.z > 0)
+    def _():
+        finish(place.z)
+
+    @pl.when(place.z < nz - 1)
+    def _():
+        finish(nz)
 
     @pl.loop(0, 2 * nz)
     def _(i):
@@ -145,7 +180,7 @@
 
     @pl.loop(0, nz - 1)
     def _(k):
-        depth_copy(k).wait_send()
+        depth_copy(k, k, 1).wait_send()
 
 
 def all_gather(place, rows, full, bufs):
@@ -155,50 +190,85 @@
     def at(block):
         return full.at[rows_of(block, rows)]
 
-    def depth_copy(k, source_z):
-        block = at(place.index(source_z, place.y, place.c))
-        return remote(block, block, zs.at[k], zr.at[k], place.depth_peer(k))
-
-    def side_copy(k, side):
-        block = at(place.index((place.z - k + nz) % nz, side, place.c))
-        return remote(block, block, ys.at[k], yr.at[k], place.side_peer())
-
-    def core_copy(i, k, side, core):
-        block = at(place.index((place.z - k + nz) % nz, side, core))
+    def depth_copy(distance, step):
+        block = at(place.index(place.z - step * (distance - 1), place.y, place.c))
+        i = distance if step == 1 else nz + distance
+        return remote(block, block, zs.at[i], zr.at[i], place.depth_peer(step))
+
+    def depth_arrived(distance, step):
+        block = at(place.index(place.z - step * distance, place.y, place.c))
+        i = distance if step == 1 else nz + distance
+        remote(block, block, zs.at[i], zr.at[i], place.depth_peer(step)).wait_recv()
+
+    def side_copy(z, side):
+        block = at(place.index(z, side, place.c))
+        return remote(block, block, ys.at[z], yr.at[z], place.side_peer())
+
+    def core_copy(i, z, side, core):
+        block = at(place.index(z, side, core))
         return remote(block, block, cs.at[i], cr.at[i], place.core_peer())
 
+    def share(z):
+        side_copy(z, place.y).start()
+        core_copy(z, z, place.y, place.c).start()
+
+    def pass_on(z):
+        side_copy(z, 1 - place.y).wait_recv()
+        core_copy(nz + z, z, 1 - place.y, place.c).start()
+
+    def has_source(distance, step):
+        return place.z >= distance if step == 1 else place.z + distance < nz
+
+    def has_next(step):
+        return place.z < nz - 1 if step == 1 else place.z > 0
+
+    for step in (1, -1):
+
+        @pl.when(has_next(step))
+        def _(step=step):
+            depth_copy(1, step).start()
+
+    share(place.z)
+
     @pl.loop(1, nz)
     def _(k):
-        depth_copy(k, place.z).start()
+        for step in (1, -1):
+
+            @pl.when(has_source(k, step))
+            def _(step=step):
+                depth_arrived(k, step)
+
+                @pl.when(has_next(step))
+                def _():
+                    depth_copy(k + 1, step).start()
+
+                share(place.z - step * k)
+
+    pass_on(place.z)
+
+    @pl.loop(1, nz)
+    def _(k):
+        for step in (1, -1):
+
+            @pl.when(has_source(k, step))
+            def _(step=step):
+                pass_on(place.z - step * k)
 
     @pl.loop(0, nz)
-    def _(k):
-        @pl.when(k > 0)
-        def _():
-            depth_copy(k, (place.z - k + nz) % nz).wait_recv()
-
-        side_copy(k, place.y).start()
-        core_copy(k, k, place.y, place.c).start()
-
-    @pl.loop(0, nz)
-    def _(k):
-        side_copy(k, 1 - place.y).wait_recv()
-        core_copy(nz + k, k, 1 - place.y, place.c).start()
-
-    @pl.loop(0, nz)
-    def _(k):
-        core_copy(k, k, place.y, 1 - place.c).wait_recv()
-        core_copy(nz + k, k, 1 - place.y, 1 - place.c).wait_recv()
-
-    @pl.loop(1, nz)
-    def _(k):
-        depth_copy(k, place.z).wait_send()
-
-    @pl.loop(0, nz)
-    def _(k):
-        side_copy(k, place.y).wait_send()
-        core_copy(k, k, place.y, place.c).wait_send()
-        core_copy(nz + k, k, 1 - place.y, place.c).wait_send()
+    def _(z):
+        core_copy(z, z, place.y, 1 - place.c).wait_recv()
+        core_copy(nz + z, z, 1 - place.y, 1 - place.c).wait_recv()
+        side_copy(z, place.y).wait_send()
+        core_copy(z, z, place.y, place.c).wait_send()
+        core_copy(nz + z, z, 1 - place.y, place.c).wait_send()
+
+    @pl.loop(0, nz - 1)
+    def _(k):
+        for step in (1, -1):
+
+            @pl.when(jnp.logical_and(jnp.logical_or(k == 0, has_source(k, step)), has_next(step)))
+            def _(step=step):
+                depth_copy(k + 1, step).wait_send()
 
 
 def lift_kernel(
@@ -217,7 +287,7 @@
         k = (s % (2 * nz)) // 2
         side = (place.y + 1 + half) % 2
         core = (place.c + 1 + s) % 2
-        return place.index((place.z + k + 1) % nz, side, core)
+        return place.index(place.depth_at(k), side, core)
 
     def query_copy(s):
         return pltpu.make_async_copy(
@@ -304,19 +374,19 @@
         pltpu.VMEM((nz, *block), jnp.bfloat16),
         pltpu.VMEM((nz, *block), jnp.bfloat16),
         pltpu.VMEM((nz - 1, *block), jnp.bfloat16),
-        pltpu.VMEM((nz - 1, *block), jnp.bfloat16),
+        pltpu.VMEM((nz + 1, *block), jnp.bfloat16),
         dma((2 * nz,)),
         dma((2 * nz,)),
         dma((nz,)),
         dma((nz,)),
         dma((nz - 1,)),
-        dma((nz - 1,)),
+        dma((nz + 1,)),
     ]
 
 
 def gather_scratch(nz):
     dma = pltpu.SemaphoreType.DMA
-    return [dma((2 * nz,)), dma((2 * nz,)), dma((nz,)), dma((nz,)), dma((nz,)), dma((nz,))]
+    return [dma((2 * nz,)), dma((2 * nz,)), dma((nz,)), dma((nz,)), dma((2 * nz,)), dma((2 * nz,))]
 
 
 def lift(n, query_grad, out_basis, in_basis, eigenvalues, damping):

time: 164 us -> 149 us (0.909); the launches traced: 161 us -> 149 us
  Pallas kernels: 143 us -> 130 us
    pallas_call x1, Pallas kernels: 143 us -> 130 us  [lift(): pl.pallas_call(functools.partial(lift_kernel, n), out_shape=jax.ShapeDtyp...]
where the time goes in v2:
time: 149 us
  Pallas kernels  130 us (87%)
  matrix products  15.8 us (11%)
  local copies, waits for them, and re-layouts  2.02 us (1%)
    pallas_call x1, Pallas kernels, lift(): pl.pallas_call(functools.partial(lift_kernel, n), out_shape=jax.ShapeDtyp...  130 us
    dot_general x1, matrix products, on_device(): lax.dot_general(lifted, in_basis, (((1,), (1,)), ((), ())), preferred_ele...  15.8 us

profile of v2, /device:TPU:0, one launch (start us, length us, event | category | flops | bytes accessed | tf_op | source)
XLA Modules:
  0.0 148.8 jit_solution(14804177128781671491)
XLA Ops:
  0.7 0.0 copy-start
  0.7 1.1 copy-done
  1.8 0.0 copy-start.2
  1.8 0.9 copy-done.2
  2.7 0.0 copy-start.1
  2.7 130.3 %shard_map.55 = bf16[8192,384]{1,0:T(8,128)(2,1)} custom-call(bf16[8192,896]{1,0:T(8,128)(2,1)} %query.1, bf16[512,2048]{1,0:T(8,128)(2,1)} %out_basis.1, bf16[896,384]{1,0:T(8,128)(2,1)S(1)} %copy-done, f32[128,384]{1,0:T(8,128)S(1)} %copy-done.2, f32[1,1]{1,0:T(1,128)} %bitcast.5.damping), custom_call_target="tpu_custom_call" | custom-call | flops 7247757312 | bytes 14680064 | tf_op jit(solution)/shard_map/pallas_call | solution.py:401
  133.0 0.0 copy-done.1
  133.0 15.8 %add_convert_fusion = bf16[8192,896]{1,0:T(8,128)(2,1)} fusion(bf16[8192,896]{1,0:T(8,128)(2,1)} %query.1, bf16[8192,384]{1,0:T(8,128)(2,1)} %shard_map.55, bf16[896,384]{1,0:T(8,128)(2,1)S(1)} %copy-done.1, f32[]{:T(128)} %bitcast.4), kind=kOutput, calls=%fused_computation | convolution fusion | flops 5666504704 | bytes 36339716 | tf_op jit(solution)/shard_map/dot_general | solution.py:431
Async XLA Ops:
  0.7 1.1 copy-start
  1.8 0.9 copy-start.2
  2.7 130.3 %copy-start.1 = (bf16[896,384]{1,0:T(8,128)(2,1)S(1)}, bf16[896,384]{1,0:T(8,128)(2,1)}, u32[]{:S(2)}) copy-start(bf16[896,384]{1,0:T(8,128)(2,1)} %in_basis.1) | copy-start | bytes 2064388

commit v3 on v2

--- a/solution.py
+++ b/solution.py
@@ -272,8 +272,9 @@
 
 
 def lift_kernel(
-    n, query, out_basis, in_basis, eigenvalues, damping, lifted,
-    slots, basis, turned, projected, scaled, slot_sems, basis_sem, *rest
+    n, query, out_basis, in_source, eigen_source, damping, lifted,
+    slots, basis, turned, projected, scaled, in_basis, eigenvalues,
+    slot_sems, basis_sem, in_sem, eigen_sem, *rest
 ):
     place = Place(n)
     nz = place.depths
@@ -295,6 +296,9 @@
         )
 
     basis_copy = pltpu.make_async_copy(out_basis, basis, basis_sem)
+    in_copy = pltpu.make_async_copy(in_source, in_basis, in_sem)
+    eigen_copy = pltpu.make_async_copy(eigen_source, eigenvalues, eigen_sem)
+    in_copy.start()
 
     @pl.loop(0, SLOTS - 1)
     def _(s):
@@ -329,9 +333,12 @@
             ).astype(out.dtype)
 
     basis_copy.start()
+    eigen_copy.start()
+    in_copy.wait()
 
     def turn():
         basis_copy.wait()
+        eigen_copy.wait()
         width = 256
         for j in range(basis.shape[1] // width):
             turned[j * width : (j + 1) * width, :] = basis[:, j * width : (j + 1) * width].T
@@ -401,7 +408,7 @@
     return pl.pallas_call(
         functools.partial(lift_kernel, n),
         out_shape=jax.ShapeDtypeStruct((height, width), jnp.bfloat16),
-        in_specs=[hbm, hbm, vmem, vmem, vmem],
+        in_specs=[hbm, hbm, hbm, hbm, vmem],
         out_specs=vmem,
         scratch_shapes=[
             pltpu.VMEM((SLOTS, rows, inner), jnp.bfloat16),
@@ -409,7 +416,11 @@
             pltpu.VMEM((kept, rows), jnp.bfloat16),
             pltpu.VMEM((rows, width), jnp.bfloat16),
             pltpu.VMEM((kept, width), jnp.bfloat16),
+            pltpu.VMEM((inner, width), jnp.bfloat16),
+            pltpu.VMEM((share, width), jnp.float32),
             pltpu.SemaphoreType.DMA((SLOTS,)),
+            pltpu.SemaphoreType.DMA,
+            pltpu.SemaphoreType.DMA,
             pltpu.SemaphoreType.DMA,
             *scatter_scratch(nz, rows, width),
             *scatter_scratch(nz, share, width),

time: 149 us -> 149 us (level)
  no operation moved by 1% of the time
where the time goes in v3:
time: 149 us
  Pallas kernels  131 us (88%)
  matrix products  15.8 us (11%)
  local copies, waits for them, and re-layouts  2.02 us (1%)
    pallas_call x1, Pallas kernels, lift(): pl.pallas_call(functools.partial(lift_kernel, n), out_shape=jax.ShapeDtyp...  131 us
    dot_general x1, matrix products, on_device(): lax.dot_general(lifted, in_basis, (((1,), (1,)), ((), ())), preferred_ele...  15.8 us

profile of v3, /device:TPU:0, one launch (start us, length us, event | category | flops | bytes accessed | tf_op | source)
XLA Modules:
  0.0 149.3 jit_solution(8589987660678200290)
XLA Ops:
  0.7 0.0 copy-start
  0.7 1.1 copy-done
  1.8 0.0 copy-start.2
  1.8 0.9 copy-done.2
  2.7 0.0 copy-start.1
  2.7 130.8 %shard_map.55 = bf16[8192,384]{1,0:T(8,128)(2,1)} custom-call(bf16[8192,896]{1,0:T(8,128)(2,1)} %query.1, bf16[512,2048]{1,0:T(8,128)(2,1)} %out_basis.1, bf16[896,384]{1,0:T(8,128)(2,1)S(1)} %copy-done, f32[128,384]{1,0:T(8,128)S(1)} %copy-done.2, f32[1,1]{1,0:T(1,128)} %bitcast.5.damping), custom_call_target="tpu_custom_call" | custom-call | flops 7247757312 | bytes 14680064 | tf_op jit(solution)/shard_map/pallas_call | solution.py:408
  133.5 0.0 copy-done.1
  133.5 15.8 %add_convert_fusion = bf16[8192,896]{1,0:T(8,128)(2,1)} fusion(bf16[8192,896]{1,0:T(8,128)(2,1)} %query.1, bf16[8192,384]{1,0:T(8,128)(2,1)} %shard_map.55, bf16[896,384]{1,0:T(8,128)(2,1)S(1)} %copy-done.1, f32[]{:T(128)} %bitcast.4), kind=kOutput, calls=%fused_computation | convolution fusion | flops 5666504704 | bytes 36339716 | tf_op jit(solution)/shard_map/dot_general | solution.py:442
Async XLA Ops:
  0.7 1.1 copy-start
  1.8 0.9 copy-start.2
  2.7 130.8 %copy-start.1 = (bf16[896,384]{1,0:T(8,128)(2,1)S(1)}, bf16[896,384]{1,0:T(8,128)(2,1)}, u32[]{:S(2)}) copy-start(bf16[896,384]{1,0:T(8,128)(2,1)} %in_source.1) | copy-start | bytes 2064388
